TPU v7x, 512 devices: a whole 4x8x8 slice. The times are simulated.
512 devices in a mesh: blk: 64 (over z_hi, x, y), uly: 8 (over z_lo, core).
Axes of the slice: x: 4, y: 8, z: 8 (z_hi: 2, z_lo: 4; z = z_hi * 4 + z_lo), core: 2. Of those that a mesh axis runs over, the one named last changes fastest.
Arguments:
- queries: bfloat16 [16384, 4096], P(('blk', 'uly')), may hold values from -40 to 40
- keys: bfloat16 [16384, 4096], P(('blk', 'uly')), may hold values from -40 to 40
- values: bfloat16 [16384, 4096], P(('blk', 'uly')), may hold values from -6 to 6
- flags: int32 [16384], P(('blk', 'uly')), may hold values from 0 to 1
- q_mask: bfloat16 [4096], replicated, may hold values from -15 to 15
- k_mask: bfloat16 [4096], replicated, may hold values from -6 to 6
- v_mask: bfloat16 [4096], replicated, may hold values from -6 to 6
Outputs:
- attended: bfloat16 [16384, 4096], P(('blk', 'uly'))
All inputs are finite; a program needn't handle non-finite values.
Results may differ from a plain program's by a relative error of at most 0.0082.
Values may be sent and summed in bfloat16 or wider, within the bound.
A program may use at most 64 MiB of HBM per device.

v0:
```python
import math

import jax
import jax.numpy as jnp
from jax import lax
from jax.sharding import PartitionSpec as P

HD = 128
GROUP = 8


rope_base = 500000.0


def partner_2(value, axis, bit):
    mask = 2**bit
    pairs = [(source, source ^ mask) for source in range(lax.axis_size(axis))]
    return lax.ppermute(value, axis, pairs)


def rotate_heads(hidden_rows, positions):
    row_count = hidden_rows.shape[0]
    half_dim = HD // 2
    split_rows = hidden_rows.astype(jnp.float32).reshape(row_count, -1, HD)
    freq_index = jnp.arange(half_dim).astype(jnp.float32)
    frequency = jnp.exp(freq_index * (-2.0 * math.log(rope_base) / HD))
    angles = positions[:, None] * frequency[None, :]
    cosine = jnp.cos(angles)[:, None, :]
    sine_part = jnp.sin(angles)[:, None, :]
    first_half = split_rows[..., :half_dim]
    second_half = split_rows[..., half_dim:]
    rotated = jnp.concatenate(
        [
            first_half * cosine - second_half * sine_part,
            second_half * cosine + first_half * sine_part,
        ],
        axis=-1,
    )
    return rotated.reshape(row_count, -1).astype(jnp.bfloat16)


def attend_piece(fold_state, key_piece, value_piece, query_block):
    row_max, row_sum, accumulated = fold_state
    heads_here = query_block.shape[1]
    key_block = key_piece.reshape(key_piece.shape[0], heads_here, HD)
    value_block = value_piece.reshape(value_piece.shape[0], heads_here, HD)
    scores = jnp.einsum(
        "rhd,khd->rhk", query_block, key_block, preferred_element_type=jnp.float32
    ) * (1.0 / math.sqrt(HD))
    new_max = jnp.maximum(row_max, jnp.max(scores, axis=2))
    correction = jnp.exp(row_max - new_max)
    weights = jnp.exp(scores - new_max[:, :, None])
    row_sum = row_sum * correction + jnp.sum(weights, axis=2)
    accumulated = accumulated * correction[:, :, None] + jnp.einsum(
        "rhk,khd->rhd",
        weights.astype(jnp.bfloat16),
        value_block,
        preferred_element_type=jnp.float32,
    )
    return (new_max, row_sum, accumulated)


def fold_pieces(fold_state, key_piece, value_piece, query_block):
    piece_rows = key_piece.shape[0]
    step_rows = piece_rows
    if piece_rows > 512:
        step_rows = 512
        while piece_rows % step_rows:
            step_rows -= 1
    turn_count = piece_rows // step_rows
    if turn_count == 1:
        return attend_piece(fold_state, key_piece, value_piece, query_block)

    def one_turn(turn_index, inner_state):
        key_part = lax.dynamic_slice_in_dim(key_piece, turn_index * step_rows, step_rows, 0)
        value_part = lax.dynamic_slice_in_dim(value_piece, turn_index * step_rows, step_rows, 0)
        return attend_piece(inner_state, key_part, value_part, query_block)

    return lax.fori_loop(0, turn_count, one_turn, fold_state)


def initial_state(block_rows, heads_here):
    return (
        jnp.full((block_rows, heads_here), -1e30, jnp.float32),
        jnp.zeros((block_rows, heads_here), jnp.float32),
        jnp.zeros((block_rows, heads_here, HD), jnp.float32),
    )


def finish_state(fold_state):
    row_max, row_sum, accumulated = fold_state
    normalized = accumulated / row_sum[:, :, None]
    return normalized.reshape(normalized.shape[0], -1).astype(jnp.bfloat16)


def body(queries, keys, values, flags, q_mask, k_mask, v_mask):
    tok_rows = queries.shape[0]
    uly_count = lax.axis_size("uly")
    within_seq = lax.axis_index("blk") % GROUP * uly_count + lax.axis_index("uly")
    positions = (within_seq * tok_rows + jnp.arange(tok_rows, dtype=jnp.int32)).astype(jnp.float32)
    masked = (flags == 1)[:, None]
    query_rot = rotate_heads(jnp.where(masked, q_mask[None, :], queries), positions)
    key_rot = rotate_heads(jnp.where(masked, k_mask[None, :], keys), positions)
    value_in = jnp.where(masked, v_mask[None, :], values)
    query_group, key_group, value_group = (
        lax.all_to_all(query_rot, "uly", split_axis=1, concat_axis=0, tiled=True),
        lax.all_to_all(key_rot, "uly", split_axis=1, concat_axis=0, tiled=True),
        lax.all_to_all(value_in, "uly", split_axis=1, concat_axis=0, tiled=True),
    )
    block_rows = query_group.shape[0]
    heads_here = query_group.shape[1] // HD
    query_block = query_group.reshape(block_rows, heads_here, HD)
    fold_state = fold_pieces(
        initial_state(block_rows, heads_here), key_group, value_group, query_block
    )
    bit_count = GROUP.bit_length() - 1
    bit_list = list(range(bit_count))
    held = jnp.stack((key_group, value_group))
    for turn, bit in enumerate(bit_list):
        partner = partner_2(held, "blk", bit)
        fold_state = fold_pieces(fold_state, partner[0], partner[1], query_block)
        if turn + 1 < len(bit_list):
            held = jnp.concatenate([held, partner], axis=1)
    attended = finish_state(fold_state)
    return lax.all_to_all(attended, "uly", split_axis=0, concat_axis=1, tiled=True)


def solution(mesh):
    placed = (
        P(("blk", "uly"), None),
        P(("blk", "uly"), None),
        P(("blk", "uly"), None),
        P(("blk", "uly")),
        P(),
        P(),
        P(),
    )
    return jax.shard_map(
        body, mesh=mesh, in_specs=placed, out_specs=P(("blk", "uly"), None), check_vma=False
    )
```

profile of v0, /device:TPU:1, one launch (start us, length us, event | category | flops | bytes accessed | tf_op | source)
XLA Modules:
  0.0 230.8 jit_solution(4039851712764261056)
XLA Ops:
  0.0 0.7 broadcast_compare_fusion
  0.7 1.3 convert_bitcast_fusion
  2.0 0.1 copy.97
  2.1 0.1 copy.98
  2.2 0.1 multiply_cosine_fusion
  2.3 0.5 subtract_convert_fusion
  2.8 0.3 pad_maximum_fusion.3
  3.1 0.2 convert_element_type.52
  3.3 0.8 copy.64
  4.1 10.2 %all-to-all-start = ((bf16[32,8,512]{2,0,1:T(8,128)(2,1)}), bf16[32,8,512]{2,0,1:T(8,128)(2,1)S(1)}, u32[]{:S(2)}, u32[]{:S(2)}) async-start(bf16[32,8,512]{2,0,1:T(8,128)(2,1)} %copy.64), calls=%async_computation | async-start | bytes 524288 | tf_op jit(solution)/shard_map/all_to_all | solution.py:107
  14.3 8.7 %all-to-all-done = bf16[32,8,512]{2,0,1:T(8,128)(2,1)S(1)} async-done(((bf16[32,8,512]{2,0,1:T(8,128)(2,1)}), bf16[32,8,512]{2,0,1:T(8,128)(2,1)S(1)}, u32[]{:S(2)}, u32[]{:S(2)}) %all-to-all-start) | async-done | bytes 262176 | tf_op jit(solution)/shard_map/all_to_all | solution.py:107
  23.0 12.1 %all_to_all.58 = bf16[32,8,512]{2,0,1:T(8,128)(2,1)S(1)} all-to-all(bf16[32,8,512]{2,0,1:T(8,128)(2,1)S(1)} %bitcast.116), channel_id=1, replica_groups=mesh['blk'=64,'uly'=8] {'uly'}, dimensions={1} | all-to-all | bytes 524288 | tf_op jit(solution)/shard_map/all_to_all | solution.py:108
  35.1 0.1 pad_maximum_fusion.2
  35.2 1.9 collective-permute-start
  37.1 0.2 convert_element_type.53
  37.3 0.8 copy.65
  38.1 4.5 %all-to-all-start.1 = ((bf16[32,8,512]{2,0,1:T(8,128)(2,1)}), bf16[32,8,512]{2,0,1:T(8,128)(2,1)S(1)}, u32[]{:S(2)}, u32[]{:S(2)}) async-start(bf16[32,8,512]{2,0,1:T(8,128)(2,1)} %copy.65), calls=%async_computation.1 | async-start | bytes 524288 | tf_op jit(solution)/shard_map/all_to_all | solution.py:106
  42.5 6.9 %collective-permute-done = bf16[2,256,512]{2,1,0:T(8,128)(2,1)S(1)} collective-permute-done((bf16[2,256,512]{2,1,0:T(8,128)(2,1)S(1)}, bf16[2,256,512]{2,1,0:T(8,128)(2,1)S(1)}, u32[]{:S(2)}, u32[]{:S(2)}) %collective-permute-start) | collective-permute-done | bytes 524320 | tf_op jit(solution)/shard_map/ppermute | solution.py:18
  49.4 1.1 pad_maximum_fusion.1
  50.6 2.8 %collective-permute-start.1 = (bf16[2,512,512]{2,1,0:T(8,128)(2,1)}, bf16[2,512,512]{2,1,0:T(8,128)(2,1)}, u32[]{:S(2)}, u32[]{:S(2)}) collective-permute-start(bf16[2,512,512]{2,1,0:T(8,128)(2,1)} %pad_maximum_fusion.1), channel_id=1, source_target_pairs={{0,16},{8,24},{16,0},{24,8},{32,48},{40,56},{48,32},{56,40},{64,80... | collective-permute-start | bytes 3145736 | tf_op jit(solution)/shard_map/ppermute | solution.py:18
  53.3 0.0 all-to-all-done.1
  53.4 0.1 reshape.164
  53.4 0.1 reshape.161
  53.5 0.1 reshape.165
  53.6 0.3 fusion.42
  53.9 0.0 copy-done
  54.0 0.8 copy.69
  54.8 0.8 copy.77
  55.7 1.3 fusion.41
  57.0 44.2 %collective-permute-done.1 = bf16[2,512,512]{2,1,0:T(8,128)(2,1)} collective-permute-done((bf16[2,512,512]{2,1,0:T(8,128)(2,1)}, bf16[2,512,512]{2,1,0:T(8,128)(2,1)}, u32[]{:S(2)}, u32[]{:S(2)}) %collective-permute-start.1) | collective-permute-done | bytes 1048608 | tf_op jit(solution)/shard_map/ppermute | solution.py:18
  101.1 2.8 %pad_maximum_fusion = bf16[2,1024,512]{2,1,0:T(8,128)(2,1)} fusion(bf16[2,512,512]{2,1,0:T(8,128)(2,1)} %collective-permute-done.1, bf16[2,256,512]{2,1,0:T(8,128)(2,1)} %copy-done, bf16[1,256,512]{2,1,0:T(8,128)(2,1)S(1)} %bitcast.108, bf16[1,256,512]{2,1,0:T(8,128)(2,1)S(1)} %bitcast.104), kind=kLoop, calls=%fused_computation.14 | loop fusion | flops 8388608 | bytes 4194304 | tf_op jit(solution)/shard_map/concatenate | solution.py:123
  103.9 6.0 %collective-permute-start.2 = (bf16[2,1024,512]{2,1,0:T(8,128)(2,1)}, bf16[2,1024,512]{2,1,0:T(8,128)(2,1)}, u32[]{:S(2)}, u32[]{:S(2)}) collective-permute-start(bf16[2,1024,512]{2,1,0:T(8,128)(2,1)} %pad_maximum_fusion), channel_id=1, source_target_pairs={{0,32},{8,40},{16,48},{24,56},{32,0},{40,8},{48,16},{56,24},{64,96... | collective-permute-start | bytes 6291464 | tf_op jit(solution)/shard_map/ppermute | solution.py:18
  109.9 2.3 fusion.39
  112.2 2.0 copy.72
  114.2 2.1 copy.79
  116.3 1.5 bitcast_reduce_fusion.1
  117.9 0.2 fusion.22
  118.0 0.2 fusion.24
  118.2 0.4 fusion.10
  118.6 0.3 fusion.15
  118.9 0.2 copy-done.2
  119.1 0.3 fusion.17
  119.5 0.2 copy-done.1
  119.7 1.3 fusion.13
  121.0 81.0 %collective-permute-done.2 = bf16[2,1024,512]{2,1,0:T(8,128)(2,1)} collective-permute-done((bf16[2,1024,512]{2,1,0:T(8,128)(2,1)}, bf16[2,1024,512]{2,1,0:T(8,128)(2,1)}, u32[]{:S(2)}, u32[]{:S(2)}) %collective-permute-start.2) | collective-permute-done | bytes 2097184 | tf_op jit(solution)/shard_map/ppermute | solution.py:18
  202.0 3.0 %slice_bitcast_fusion = (bf16[1024,512]{1,0:T(8,128)(2,1)}, bf16[1024,512]{1,0:T(8,128)(2,1)}) fusion(bf16[2,1024,512]{2,1,0:T(8,128)(2,1)} %collective-permute-done.2), kind=kLoop, calls=%fused_computation.32 | loop fusion | bytes 4194304 | tf_op jit(solution)/shard_map/squeeze | solution.py:121
  205.0 10.0 %while.17 = (s32[]{:T(128)}, f32[256,4]{0,1:T(4,128)S(1)}, f32[256,4]{0,1:T(4,128)S(1)}, f32[256,4,128]{0,2,1:T(8,128)}, bf16[1024,512]{1,0:T(8,128)(2,1)}, /*in...) while((s32[]{:T(128)}, f32[256,4]{0,1:T(4,128)S(1)}, ...), condition=%wide.region_9.10_spmd, body=%wide.region_6.9_spmd.sunk | while | flops 272893952 | bytes 12910751 | solution.py:79
  205.0 1.3 constant_dynamic-slice_fusion.3
  206.3 0.2 copy.121
  206.5 0.5 bitcast_reduce_fusion.3
  207.0 0.4 fusion.60
  207.4 0.2 copy.122
  207.6 2.4 %fusion.61 = f32[256,4,128]{0,2,1:T(8,128)} fusion(bf16[512,4,128]{0,2,1:T(8,128)(2,1)S(1)} %bitcast.99, f32[4,512,256]{2,1,0:T(8,128)S(1)} %get-tuple-element.256, f32[256,4]{0,1:T(4,128)S(1)} %max.39, f32[256,4,128]{0,2,1:T(8,128)} %get-tuple-element.274, f32[256,4]{0,1:T(4,128)S(1)} %get-tuple-element.259), kind=kOutput, calls=%fused_computation.6.clone.1 | convolution fusion | flops 136052736 | bytes 3678208 | tf_op jit(solution)/shard_map/while/body/eval_jaxpr/rhk,khd->rhd/dot_general | solution.py:54
  210.0 1.3 constant_dynamic-slice_fusion.3
  211.3 0.2 copy.121
  211.5 0.5 bitcast_reduce_fusion.3
  212.0 0.4 fusion.60
  212.4 0.2 copy.122
  212.6 2.4 %fusion.61 = f32[256,4,128]{0,2,1:T(8,128)} fusion(bf16[512,4,128]{0,2,1:T(8,128)(2,1)S(1)} %bitcast.99, f32[4,512,256]{2,1,0:T(8,128)S(1)} %get-tuple-element.256, f32[256,4]{0,1:T(4,128)S(1)} %max.39, f32[256,4,128]{0,2,1:T(8,128)} %get-tuple-element.274, f32[256,4]{0,1:T(4,128)S(1)} %get-tuple-element.259), kind=kOutput, calls=%fused_computation.6.clone.1 | convolution fusion | flops 136052736 | bytes 3678208 | tf_op jit(solution)/shard_map/while/body/eval_jaxpr/rhk,khd->rhd/dot_general | solution.py:54
  215.0 1.1 divide_convert_fusion
  216.0 0.2 copy.84
  216.2 0.1 convert_element_type.58
  216.3 13.7 %all_to_all.59 = bf16[8,32,512]{2,1,0:T(8,128)(2,1)S(1)} all-to-all(bf16[8,32,512]{2,1,0:T(8,128)(2,1)S(1)} %convert_element_type.58), channel_id=1, replica_groups=mesh['blk'=64,'uly'=8] {'uly'}, dimensions={0} | all-to-all | bytes 524288 | tf_op jit(solution)/shard_map/all_to_all | solution.py:125
  230.0 0.7 copy.96
  (16 shorter events, 0.2 us)
Async XLA Ops:
  4.1 18.9 %all-to-all-start = ((bf16[32,8,512]{2,0,1:T(8,128)(2,1)}), bf16[32,8,512]{2,0,1:T(8,128)(2,1)S(1)}, u32[]{:S(2)}, u32[]{:S(2)}) async-start(bf16[32,8,512]{2,0,1:T(8,128)(2,1)} %copy.64), calls=%async_computation | async-start | bytes 524288 | tf_op jit(solution)/shard_map/all_to_all | solution.py:107
  35.2 14.3 %collective-permute-start = (bf16[2,256,512]{2,1,0:T(8,128)(2,1)S(1)}, bf16[2,256,512]{2,1,0:T(8,128)(2,1)S(1)}, u32[]{:S(2)}, u32[]{:S(2)}) collective-permute-start(bf16[2,256,512]{2,1,0:T(8,128)(2,1)S(1)} %pad_maximum_fusion.2), channel_id=1, source_target_pairs={{0,8},{8,0},{16,24},{24,16},{32,40},{40,32},{48,56},{56,48},{64,72... | collective-permute-start | bytes 1572872 | tf_op jit(solution)/shard_map/ppermute | solution.py:18
  38.1 15.3 %all-to-all-start.1 = ((bf16[32,8,512]{2,0,1:T(8,128)(2,1)}), bf16[32,8,512]{2,0,1:T(8,128)(2,1)S(1)}, u32[]{:S(2)}, u32[]{:S(2)}) async-start(bf16[32,8,512]{2,0,1:T(8,128)(2,1)} %copy.65), calls=%async_computation.1 | async-start | bytes 524288 | tf_op jit(solution)/shard_map/all_to_all | solution.py:106
  49.4 4.5 %copy-start = (bf16[2,256,512]{2,1,0:T(8,128)(2,1)}, bf16[2,256,512]{2,1,0:T(8,128)(2,1)S(1)}, u32[]{:S(2)}) copy-start(bf16[2,256,512]{2,1,0:T(8,128)(2,1)S(1)} %collective-permute-done) | copy-start | bytes 1572868
  50.6 50.6 %collective-permute-start.1 = (bf16[2,512,512]{2,1,0:T(8,128)(2,1)}, bf16[2,512,512]{2,1,0:T(8,128)(2,1)}, u32[]{:S(2)}, u32[]{:S(2)}) collective-permute-start(bf16[2,512,512]{2,1,0:T(8,128)(2,1)} %pad_maximum_fusion.1), channel_id=1, source_target_pairs={{0,16},{8,24},{16,0},{24,8},{32,48},{40,56},{48,32},{56,40},{64,80... | collective-permute-start | bytes 3145736 | tf_op jit(solution)/shard_map/ppermute | solution.py:18
  103.9 98.1 %collective-permute-start.2 = (bf16[2,1024,512]{2,1,0:T(8,128)(2,1)}, bf16[2,1024,512]{2,1,0:T(8,128)(2,1)}, u32[]{:S(2)}, u32[]{:S(2)}) collective-permute-start(bf16[2,1024,512]{2,1,0:T(8,128)(2,1)} %pad_maximum_fusion), channel_id=1, source_target_pairs={{0,32},{8,40},{16,48},{24,56},{32,0},{40,8},{48,16},{56,24},{64,96... | collective-permute-start | bytes 6291464 | tf_op jit(solution)/shard_map/ppermute | solution.py:18
  118.2 1.0 copy-start.2
  118.6 1.1 copy-start.1
where the time goes:
time: 232 us; the launch traced here: 231 us
  waiting for transfers between devices  141 us (61%)
  blocking collectives  25.8 us (11%)
  starting transfers between devices  25.3 us (11%)
  local copies, waits for them, and re-layouts  18.2 us (8%)
  matrix products  10.9 us (5%)
  other arithmetic  9.43 us (4%)
    ppermute x3, waiting for transfers between devices, partner_2(): return lax.ppermute(value, axis, pairs)  132 us
    all_to_all x1, blocking collectives, body(): lax.all_to_all(attended, 'uly', split_axis=0, concat_axis=1, tiled=True)  13.7 us
    all_to_all x1, blocking collectives, body(): lax.all_to_all(value_in, 'uly', split_axis=1, concat_axis=0, tiled=True)  12.1 us
    ppermute x3, starting transfers between devices, partner_2(): return lax.ppermute(value, axis, pairs)  10.6 us
    all_to_all x1, starting transfers between devices, body(): lax.all_to_all(key_rot, 'uly', split_axis=1, concat_axis=0, tiled=True)  10.2 us
    all_to_all x1, waiting for transfers between devices, body(): lax.all_to_all(key_rot, 'uly', split_axis=1, concat_axis=0, tiled=True)  8.7 us
    slice x6, local copies, waits for them, and re-layouts, body(): fold_state = fold_pieces(fold_state, partner[0], partner[1], query_block)  8.12 us
    dot_general x5, matrix products, attend_piece(): jnp.einsum('rhk,khd->rhd', weights.astype(jnp.bfloat16), value_block, pre...  6.72 us
  transfers between devices with their start and end apart: 5, of which 4 were waited for; matrix products, arithmetic and copies ran while one was open for 7% of the time, Pallas kernels for 0%

commit v1 on v0

v1 whole, which is shorter than its diff:
```python
import functools
import math

import jax
import jax.numpy as jnp
import numpy as np
from jax import lax
from jax.experimental import pallas as pl
from jax.experimental.pallas import tpu as pltpu
from jax.sharding import PartitionSpec as P

HD = 128
ROPE_BASE = 500000.0
NY, NZ = 8, 4
CHIPS = NY * NZ
MESH = pl.DeviceIdType.MESH
SCALE = math.log2(math.e) / math.sqrt(HD)


def kernel(rows, q_hbm, k_hbm, v_hbm, flags_hbm, qm_hbm, km_hbm, vm_hbm, freq_hbm, out_ref,
           q_in, k_in, v_in, flags_ref, qm_ref, km_ref, vm_ref, freq_ref, masks, kv_stage, q_stage, kv_buf, q_buf, o_stage, o_buf,
           in_sem, kv_send, q_send, fwd_send, o_send, kv_recv, q_recv, fwd_recv, o_recv):
    blk, uly = lax.axis_index("blk"), lax.axis_index("uly")
    blk0, y, z, core = blk // NY * NY, blk % NY, uly // 2, uly % 2
    here = y * NZ + z
    sibling = (blk, z * 2 + 1 - core)
    half = CHIPS * rows
    own_slot = (NY - 1) * NZ

    def device(chip):
        return (blk0 + chip // NZ, chip % NZ * 2 + core)

    def kv_dy(i):
        j = i // NZ
        return (j // 2 + 1) * (1 - 2 * (j % 2)) * (1 - j // (NY - 1))

    def q_dy(i):
        j = i // NZ
        return (NY // 2 - (j + 1) // 2) * (1 - 2 * (j % 2))

    def ahead(dy, dz):
        return (y + dy + NY) % NY * NZ + (z + dz) % NZ

    def behind(dy, dz):
        return (y - dy + NY) % NY * NZ + (z - dz + NZ) % NZ

    barrier = pltpu.get_barrier_semaphore()

    def greet(i, carry):
        pl.semaphore_signal(barrier, inc=1, device_id=device((here + i) % CHIPS), device_id_type=MESH)
        return carry

    lax.fori_loop(1, CHIPS, greet, 0)
    pl.semaphore_signal(barrier, inc=1, device_id=sibling, device_id_type=MESH)

    loads = [
        pltpu.make_async_copy(src, dst, in_sem.at[i])
        for i, (src, dst) in enumerate((
            (freq_hbm, freq_ref), (flags_hbm, flags_ref), (qm_hbm, qm_ref), (km_hbm, km_ref), (vm_hbm, vm_ref),
            (k_hbm, k_in), (v_hbm, v_in), (q_hbm, q_in),
        ))
    ]
    for load in loads:
        load.start()
    for load in loads[:5]:
        load.wait()

    row = lax.broadcasted_iota(jnp.int32, (rows, HD), 0)
    lane = lax.broadcasted_iota(jnp.int32, (rows, HD), 1)
    position = ((y * (NZ * 2) + uly) * rows + row).astype(jnp.float32)
    angle = position * freq_ref[...]
    cosine = jnp.cos(angle)
    sine = jnp.where(lane < HD // 2, -jnp.sin(angle), jnp.sin(angle))
    diagonal = lax.broadcasted_iota(jnp.int32, (rows, rows), 0) == lax.broadcasted_iota(jnp.int32, (rows, rows), 1)
    flag_column = jnp.sum(
        jnp.where(diagonal, flags_ref[...].astype(jnp.float32), 0.0), axis=1, keepdims=True
    )
    masked = jnp.broadcast_to(flag_column, (rows, HD)) == 1.0

    for i, m_ref in enumerate((qm_ref, km_ref, vm_ref)):
        masks[i] = m_ref[...].astype(jnp.float32)

    def picked(x_in, which, chip):
        x = x_in[:, pl.ds(pl.multiple_of(chip * HD, HD), HD)].astype(jnp.float32)
        return jnp.where(masked, masks[which, pl.ds(chip, 1), :], x)

    def rotated(x):
        return (x * cosine + pltpu.roll(x, HD // 2, 1) * sine).astype(jnp.bfloat16)

    loads[5].wait()
    loads[6].wait()

    def prepare_kv(chip, carry):
        kv_stage[chip, 0] = rotated(picked(k_in, 1, chip))
        kv_stage[chip, 1] = picked(v_in, 2, chip).astype(jnp.bfloat16)
        return carry

    lax.fori_loop(0, CHIPS, prepare_kv, 0)
    loads[7].wait()

    def prepare_q(chip, carry):
        q_stage[chip] = rotated(picked(q_in, 0, chip))
        return carry

    lax.fori_loop(0, CHIPS, prepare_q, 0)

    pl.semaphore_wait(barrier, CHIPS)

    def slot(i):
        return pl.ds(pl.multiple_of(i * rows, rows), rows)

    per_kv, per_q = CHIPS // 4, CHIPS // 4

    def send_kv(i, carry):
        chip = ahead(kv_dy(i), i % NZ)
        pltpu.make_async_remote_copy(
            kv_stage.at[chip], kv_buf.at[:, slot(i)], kv_send, kv_recv.at[i // per_kv],
            device_id=device(chip), device_id_type=MESH,
        ).start()
        return carry

    lax.fori_loop(0, own_slot, send_kv, 0)
    pltpu.make_async_copy(kv_stage.at[here], kv_buf.at[:, slot(own_slot)], kv_recv.at[own_slot // per_kv]).start()
    lax.fori_loop(own_slot + 1, CHIPS, send_kv, 0)

    def send_q(i, carry):
        chip = ahead(q_dy(i), i % NZ)
        pltpu.make_async_remote_copy(
            q_stage.at[chip], q_buf.at[slot(i)], q_send, q_recv.at[i // per_q],
            device_id=device(chip), device_id_type=MESH,
        ).start()
        return carry

    lax.fori_loop(0, own_slot, send_q, 0)
    pltpu.make_async_copy(q_stage.at[here], q_buf.at[slot(own_slot)], q_recv.at[own_slot // per_q]).start()
    lax.fori_loop(own_slot + 1, CHIPS, send_q, 0)

    def drain(ref, sem):
        pltpu.make_async_copy(ref, ref, sem).wait()

    kv_rows = per_kv * rows
    for g in range(4):
        part = pl.ds(g * kv_rows, kv_rows)
        drain(kv_buf.at[:, part], kv_recv.at[g])
        pltpu.make_async_remote_copy(
            kv_buf.at[:, part], kv_buf.at[:, pl.ds(half + g * kv_rows, kv_rows)], fwd_send, fwd_recv,
            device_id=sibling, device_id_type=MESH,
        ).start()
    drain(kv_buf.at[:, pl.ds(half, half)], fwd_recv)

    q_rows = per_q * rows

    def return_o(i, carry):
        chip = behind(q_dy(i), i % NZ)
        pltpu.make_async_remote_copy(
            o_stage.at[slot(i)], o_buf.at[here], o_send, o_recv,
            device_id=device(chip), device_id_type=MESH,
        ).start()
        return carry

    def attend(g, carry):
        part = pl.ds(pl.multiple_of(g * q_rows, q_rows), q_rows)
        drain(q_buf.at[part], q_recv.at[g])
        scores = lax.dot_general(
            q_buf[part, :], kv_buf[0], (((1,), (1,)), ((), ())), preferred_element_type=jnp.float32
        )
        top = jnp.max(scores, axis=1, keepdims=True)
        weights = jnp.exp2((scores - top) * SCALE)
        total = jnp.sum(weights, axis=1, keepdims=True)
        mixture = jnp.dot(weights.astype(jnp.bfloat16), kv_buf[1], preferred_element_type=jnp.float32)
        o_stage[part, :] = (mixture / total).astype(jnp.bfloat16)
        return carry

    def attend_and_return(g, carry):
        attend(g, carry)
        lax.fori_loop(g * per_q, (g + 1) * per_q, return_o, 0)
        return carry

    lax.fori_loop(0, 3, attend_and_return, 0)
    attend(3, 0)
    lax.fori_loop(3 * per_q, own_slot, return_o, 0)
    pltpu.make_async_copy(o_stage.at[slot(own_slot)], o_buf.at[here], o_recv).start()
    lax.fori_loop(own_slot + 1, CHIPS, return_o, 0)

    others = CHIPS - 1
    drain(kv_stage.at[pl.ds(0, others)], kv_send)
    drain(q_stage.at[pl.ds(0, others)], q_send)
    drain(kv_buf.at[:, pl.ds(0, half)], fwd_send)
    drain(o_buf, o_recv)
    for head in range(CHIPS):
        out_ref[:, head * HD:(head + 1) * HD] = o_buf[head]
    drain(o_stage.at[pl.ds(0, others * rows)], o_send)


def body(queries, keys, values, flags, q_mask, k_mask, v_mask):
    rows, width = queries.shape
    half = CHIPS * rows
    pair_lanes = np.arange(HD) % (HD // 2)
    freq = np.exp(pair_lanes * (-2.0 * math.log(ROPE_BASE) / HD)).astype(np.float32)[None, :]
    vmem = pl.BlockSpec(memory_space=pltpu.VMEM)
    hbm = pl.BlockSpec(memory_space=pltpu.HBM)
    return pl.pallas_call(
        functools.partial(kernel, rows),
        out_shape=jax.ShapeDtypeStruct((rows, width), jnp.bfloat16),
        in_specs=[hbm] * 8,
        out_specs=vmem,
        scratch_shapes=[
            pltpu.VMEM((rows, width), jnp.bfloat16),
            pltpu.VMEM((rows, width), jnp.bfloat16),
            pltpu.VMEM((rows, width), jnp.bfloat16),
            pltpu.VMEM((1, rows), jnp.int32),
            pltpu.VMEM((CHIPS, HD), jnp.bfloat16),
            pltpu.VMEM((CHIPS, HD), jnp.bfloat16),
            pltpu.VMEM((CHIPS, HD), jnp.bfloat16),
            pltpu.VMEM((1, HD), jnp.float32),
            pltpu.VMEM((3, CHIPS, HD), jnp.float32),
            pltpu.VMEM((CHIPS, 2, rows, HD), jnp.bfloat16),
            pltpu.VMEM((CHIPS, rows, HD), jnp.bfloat16),
            pltpu.VMEM((2, 2 * half, HD), jnp.bfloat16),
            pltpu.VMEM((half, HD), jnp.bfloat16),
            pltpu.VMEM((half, HD), jnp.bfloat16),
            pltpu.VMEM((CHIPS, rows, HD), jnp.bfloat16),
            pltpu.SemaphoreType.DMA((8,)),
            pltpu.SemaphoreType.DMA,
            pltpu.SemaphoreType.DMA,
            pltpu.SemaphoreType.DMA,
            pltpu.SemaphoreType.DMA,
            pltpu.SemaphoreType.DMA((4,)),
            pltpu.SemaphoreType.DMA((4,)),
            pltpu.SemaphoreType.DMA,
            pltpu.SemaphoreType.DMA,
        ],
        compiler_params=pltpu.CompilerParams(
            collective_id=0, has_side_effects=True, vmem_limit_bytes=64 * 2**20
        ),
        name="attend_plane",
    )(
        queries, keys, values, flags.reshape(1, rows),
        q_mask.reshape(CHIPS, HD), k_mask.reshape(CHIPS, HD), v_mask.reshape(CHIPS, HD), jnp.asarray(freq),
    )


def solution(mesh):
    placed = (
        P(("blk", "uly"), None),
        P(("blk", "uly"), None),
        P(("blk", "uly"), None),
        P(("blk", "uly")),
        P(),
        P(),
        P(),
    )
    return jax.shard_map(
        body, mesh=mesh, in_specs=placed, out_specs=P(("blk", "uly"), None), check_vma=False
    )
```

time: 232 us -> 47.4 us (0.20)
  waiting for transfers between devices: 141 us -> 0 us
  Pallas kernels: 0 us -> 45.6 us
  blocking collectives: 25.8 us -> 0 us
  starting transfers between devices: 25.3 us -> 0 us
  local copies, waits for them, and re-layouts: 18.2 us -> 1.67 us
  matrix products: 10.9 us -> 0 us
  other arithmetic: 9.43 us -> 0 us
    ppermute x3 -> x0, waiting for transfers between devices: 132 us -> none  [partner_2(): return lax.ppermute(value, axis, pairs)]
    pallas_call x0 -> x1, Pallas kernels: none -> 45.6 us  [body(): pl.pallas_call(functools.partial(kernel, rows), out_shape=jax.ShapeDtypeS...]
    all_to_all x2 -> x0, blocking collectives: 25.8 us -> none  [the longest x1 13.7 us: body(): lax.all_to_all(attended, 'uly', split_axis=0, concat_axis=1, tiled=True)]
    all_to_all x2 -> x0, starting transfers between devices: 14.7 us -> none  [the longest x1 10.2 us: body(): lax.all_to_all(key_rot, 'uly', split_axis=1, concat_axis=0, tiled=True)]
    dot_general x10 -> x0, matrix products: 10.9 us -> none  [the longest x5 6.72 us: attend_piece(): jnp.einsum('rhk,khd->rhd', weights.astype(jnp.bfloat16), value_block, pre...]
    ppermute x3 -> x0, starting transfers between devices: 10.6 us -> none  [partner_2(): return lax.ppermute(value, axis, pairs)]
    all_to_all x2 -> x0, waiting for transfers between devices: 8.71 us -> none  [the longest x1 8.7 us: body(): lax.all_to_all(key_rot, 'uly', split_axis=1, concat_axis=0, tiled=True)]
    slice x6 -> x0, local copies, waits for them, and re-layouts: 8.12 us -> none  [body(): fold_state = fold_pieces(fold_state, partner[0], partner[1], query_block)]
  transfers between devices with their start and end apart: 5 -> 0, of which waited for: 4 -> 0; matrix products, arithmetic and copies ran while one was open for 7% -> 0% of each run, Pallas kernels for 0% -> 0%
where the time goes in v1:
time: 47.4 us; the launch traced here: 47.3 us
  Pallas kernels  45.6 us (96%)
  local copies, waits for them, and re-layouts  1.67 us (4%)
    pallas_call x1, Pallas kernels, body(): pl.pallas_call(functools.partial(kernel, rows), out_shape=jax.ShapeDtypeS...  45.6 us
    unnamed x1, local copies, waits for them, and re-layouts  1.67 us

profile of v1, /device:TPU:1, one launch (start us, length us, event | category | flops | bytes accessed | tf_op | source)
XLA Modules:
  0.0 47.3 jit_solution(8821895317516362736)
XLA Ops:
  0.0 45.6 %attend_plane.1 = bf16[32,4096]{1,0:T(8,128)(2,1)} custom-call(bf16[32,4096]{1,0:T(8,128)(2,1)} %q_hbm.1, bf16[32,4096]{1,0:T(8,128)(2,1)} %k_hbm.1, bf16[32,4096]{1,0:T(8,128)(2,1)} %v_hbm.1, s32[1,32]{1,0:T(1,128)} %bitcast.7, bf16[32,128]{1,0:T(8,128)(2,1)} %bitcast.4, bf16[32,128]{1,0:T(8,128)(2,1)} %bitcast.5, bf16[32,128]{1,0:T(8,128)(2,1)} %bitcast.6, ...), custom_call_target="tpu_custom_call" | custom-call | tf_op jit(solution)/shard_map/attend_plane/pallas_call | solution.py:202
  45.6 1.7 %copy.10 = bf16[32,4096]{1,0:T(8,128)(2,1)} copy(bf16[32,4096]{1,0:T(8,128)(2,1)} %attend_plane.1) | data formatting | bytes 524288

commit v2 on v1

v2 whole, which is shorter than its diff:
```python
import functools
import math

import jax
import jax.numpy as jnp
import numpy as np
from jax import lax
from jax.experimental import pallas as pl
from jax.experimental.pallas import tpu as pltpu
from jax.sharding import PartitionSpec as P

HD = 128
ROPE_BASE = 500000.0
NY, NZ = 8, 4
CHIPS = NY * NZ
MESH = pl.DeviceIdType.MESH
NEAR = (0, 1, 7, 2, 6, 3, 5, 4)
FAR = NEAR[::-1]
KV_ORDER = sorted([(dy, dz) for dy in range(NY) for dz in range(NZ)], key=lambda d: (min(d[0], NY - d[0]) + d[1], d))
Q_ORDER = sorted([(dy, dz) for dy in range(NY) for dz in range(NZ)], key=lambda d: (min(d[0], NY - d[0]) + d[1], d))
SENDS = [("kv", dy, dz) for dy, dz in KV_ORDER] + [("q", dy, dz) for dy, dz in Q_ORDER]
SCALE = math.log2(math.e) / math.sqrt(HD)


def kernel(rows, q_hbm, k_hbm, v_hbm, flags_hbm, qm_hbm, km_hbm, vm_hbm, base_hbm, step_hbm, out_ref,
           q_in, k_in, v_in, flags_ref, qm_ref, km_ref, vm_ref, base_ref, step_ref, masks, kv_stage, q_stage, kv_buf, q_buf, o_stage, o_buf,
           in_sem, kv_send, q_send, fwd_send, o_send, kv_recv, q_recv, fwd_recv, o_recv, ready):
    blk, uly = lax.axis_index("blk"), lax.axis_index("uly")
    blk0, y, z, core = blk // NY * NY, blk % NY, uly // 2, uly % 2
    here = y * NZ + z
    sibling = (blk, z * 2 + 1 - core)
    half = CHIPS * rows

    place = z * NY + y
    y_at = [y] + [jnp.where(y + d >= NY, y + d - NY, y + d) for d in range(1, NY)]
    z_at = [z, z + 1 - 2 * (z % 2), z + 2 - 4 * (z // 2), NZ - 1 - z]

    def turn_of(cy, cz):
        away = jnp.minimum(cy, NY - cy)
        late = jnp.where(cy + cz + blk0 + core == 0, 7, 0)
        return (2 * cz + away + late) * CHIPS + cz * NY + cy

    my_turn = turn_of(y, z)
    chips = [(cy, cz) for cz in range(NZ) for cy in range(NY)]
    turns = [turn_of(cy, cz) for cy, cz in chips]
    barrier = pltpu.get_barrier_semaphore()
    for (cy, cz), turn in zip(chips, turns):
        @pl.when(turn > my_turn)
        def _():
            pl.semaphore_signal(barrier, inc=1, device_id=(blk0 + cy, cz * 2 + core), device_id_type=MESH)

    @pl.when(core == 1)
    def _():
        pl.semaphore_signal(barrier, inc=1, device_id=sibling, device_id_type=MESH)

    loads = [
        pltpu.make_async_copy(src, dst, in_sem.at[i])
        for i, (src, dst) in enumerate((
            (base_hbm.at[y * (NZ * 2) + uly], base_ref), (step_hbm, step_ref), (flags_hbm, flags_ref), (qm_hbm, qm_ref), (km_hbm, km_ref), (vm_hbm, vm_ref),
            (k_hbm, k_in), (v_hbm, v_in), (q_hbm, q_in),
        ))
    ]
    for load in loads:
        load.start()

    entered = 1 - core
    for turn in turns:
        entered = entered + jnp.where(turn < my_turn, 1, 0)
    @pl.when(entered > 0)
    def _():
        pl.semaphore_wait(barrier, entered)

    for (cy, cz), turn in zip(chips, turns):
        @pl.when(turn < my_turn)
        def _():
            pl.semaphore_signal(ready.at[here], inc=1, device_id=(blk0 + cy, cz * 2 + core), device_id_type=MESH)

    @pl.when(core == 0)
    def _():
        pl.semaphore_signal(ready.at[here], inc=1, device_id=sibling, device_id_type=MESH)

    for load in loads[:6]:
        load.wait()

    lane = lax.broadcasted_iota(jnp.int32, (rows, HD), 1)
    turn, offset = base_ref[...], step_ref[...]
    cosine = turn[0:1] * offset[0] - turn[1:2] * offset[1]
    sine = turn[1:2] * offset[0] + turn[0:1] * offset[1]
    sine = jnp.where(lane < HD // 2, -sine, sine)
    diagonal = lax.broadcasted_iota(jnp.int32, (rows, rows), 0) == lax.broadcasted_iota(jnp.int32, (rows, rows), 1)
    flag_column = jnp.sum(
        jnp.where(diagonal, flags_ref[...].astype(jnp.float32), 0.0), axis=1, keepdims=True
    )
    masked = jnp.broadcast_to(flag_column, (rows, HD)) == 1.0

    for i, m_ref in enumerate((qm_ref, km_ref, vm_ref)):
        masks[i] = m_ref[...].astype(jnp.float32)

    def picked(x_in, which, chip):
        x = x_in[:, chip * HD:(chip + 1) * HD].astype(jnp.float32)
        return jnp.where(masked, masks[which, chip:chip + 1, :], x)

    def rotated(x):
        return (x * cosine + pltpu.roll(x, HD // 2, 1) * sine).astype(jnp.bfloat16)

    loads[6].wait()
    loads[7].wait()

    for chip in range(CHIPS):
        kv_stage[chip, 0] = rotated(picked(k_in, 1, chip))
        kv_stage[chip, 1] = picked(v_in, 2, chip).astype(jnp.bfloat16)
    loads[8].wait()
    for chip in range(CHIPS):
        q_stage[chip] = rotated(picked(q_in, 0, chip))

    def slot(i):
        return pl.ds(pl.multiple_of(i * rows, rows), rows)

    def peer(dy, dz):
        return y_at[dy] * NZ + z_at[dz], (blk0 + y_at[dy], z_at[dz] * 2 + core)

    def send_kv(dy, dz):
        chip, device = peer(dy, dz)
        pltpu.make_async_remote_copy(
            kv_stage.at[chip], kv_buf.at[:, slot(place)], kv_send, kv_recv.at[z],
            device_id=device, device_id_type=MESH,
        ).start()

    def send_q(dy, dz):
        chip, device = peer(dy, dz)
        if dy + dz:
            pltpu.make_async_remote_copy(
                q_stage.at[chip], q_buf.at[slot(place)], q_send, q_recv.at[z],
                device_id=device, device_id_type=MESH,
            ).start()
        else:
            pltpu.make_async_copy(q_stage.at[here], q_buf.at[slot(place)], q_recv.at[z]).start()

    pltpu.make_async_copy(kv_stage.at[here], kv_buf.at[:, slot(place)], kv_recv.at[z]).start()
    for dy, dz in KV_ORDER:
        @pl.when(turn_of(y_at[dy], z_at[dz]) < my_turn)
        def _():
            send_kv(dy, dz)

    for dy, dz in KV_ORDER:
        @pl.when(turn_of(y_at[dy], z_at[dz]) > my_turn)
        def _():
            pl.semaphore_wait(ready.at[peer(dy, dz)[0]], 1)
            send_kv(dy, dz)

    for dy, dz in Q_ORDER:
        send_q(dy, dz)

    def drain(ref, sem):
        pltpu.make_async_copy(ref, ref, sem).wait()

    group = NY * rows

    @pl.when(core == 1)
    def _():
        pl.semaphore_wait(ready.at[here], 1)

    for g in range(NZ):
        part = pl.ds(g * group, group)
        drain(kv_buf.at[:, part], kv_recv.at[g])
        pltpu.make_async_remote_copy(
            kv_buf.at[:, part], kv_buf.at[:, pl.ds(half + g * group, group)], fwd_send, fwd_recv,
            device_id=sibling, device_id_type=MESH,
        ).start()
    drain(kv_buf.at[:, pl.ds(half, half)], fwd_recv)

    for g in range(NZ):
        part = pl.ds(g * group, group)
        drain(q_buf.at[part], q_recv.at[g])
        scores = lax.dot_general(
            q_buf[part, :], kv_buf[0], (((1,), (1,)), ((), ())), preferred_element_type=jnp.float32
        )
        top = jnp.max(scores, axis=1, keepdims=True)
        weights = jnp.exp2((scores - top) * SCALE)
        total = jnp.sum(weights, axis=1, keepdims=True)
        mixture = jnp.dot(weights.astype(jnp.bfloat16), kv_buf[1], preferred_element_type=jnp.float32)
        o_stage[part, :] = (mixture / total).astype(jnp.bfloat16)
        for dy in FAR:
            back = functools.partial(
                pltpu.make_async_remote_copy, o_stage.at[slot(g * NY + y_at[dy])], o_buf.at[here], o_send, o_recv,
                device_id=(blk0 + y_at[dy], g * 2 + core), device_id_type=MESH,
            )
            if dy:
                back().start()
            else:
                @pl.when(z != g)
                def _():
                    back().start()

                @pl.when(z == g)
                def _():
                    pltpu.make_async_copy(o_stage.at[slot(place)], o_buf.at[here], o_recv).start()

    others = CHIPS - 1
    drain(kv_stage.at[pl.ds(0, others)], kv_send)
    drain(q_stage.at[pl.ds(0, others)], q_send)
    drain(kv_buf.at[:, pl.ds(0, half)], fwd_send)
    drain(o_buf, o_recv)
    for head in range(CHIPS):
        out_ref[:, head * HD:(head + 1) * HD] = o_buf[head]
    drain(o_stage.at[pl.ds(0, others * rows)], o_send)


def body(queries, keys, values, flags, q_mask, k_mask, v_mask):
    rows, width = queries.shape
    half = CHIPS * rows
    pair_lanes = np.arange(HD) % (HD // 2)
    freq = np.exp(pair_lanes * (-2.0 * math.log(ROPE_BASE) / HD)).astype(np.float32).astype(np.float64)
    base = np.arange(NY * NZ * 2)[:, None] * rows * freq
    step = np.arange(rows)[:, None] * freq
    base = np.stack([np.cos(base), np.sin(base)], axis=1).astype(np.float32)
    step = np.stack([np.cos(step), np.sin(step)]).astype(np.float32)
    vmem = pl.BlockSpec(memory_space=pltpu.VMEM)
    hbm = pl.BlockSpec(memory_space=pltpu.HBM)
    return pl.pallas_call(
        functools.partial(kernel, rows),
        out_shape=jax.ShapeDtypeStruct((rows, width), jnp.bfloat16),
        in_specs=[hbm] * 9,
        out_specs=vmem,
        scratch_shapes=[
            pltpu.VMEM((rows, width), jnp.bfloat16),
            pltpu.VMEM((rows, width), jnp.bfloat16),
            pltpu.VMEM((rows, width), jnp.bfloat16),
            pltpu.VMEM((1, rows), jnp.int32),
            pltpu.VMEM((CHIPS, HD), jnp.bfloat16),
            pltpu.VMEM((CHIPS, HD), jnp.bfloat16),
            pltpu.VMEM((CHIPS, HD), jnp.bfloat16),
            pltpu.VMEM((2, HD), jnp.float32),
            pltpu.VMEM((2, rows, HD), jnp.float32),
            pltpu.VMEM((3, CHIPS, HD), jnp.float32),
            pltpu.VMEM((CHIPS, 2, rows, HD), jnp.bfloat16),
            pltpu.VMEM((CHIPS, rows, HD), jnp.bfloat16),
            pltpu.VMEM((2, 2 * half, HD), jnp.bfloat16),
            pltpu.VMEM((half, HD), jnp.bfloat16),
            pltpu.VMEM((half, HD), jnp.bfloat16),
            pltpu.VMEM((CHIPS, rows, HD), jnp.bfloat16),
            pltpu.SemaphoreType.DMA((9,)),
            pltpu.SemaphoreType.DMA,
            pltpu.SemaphoreType.DMA,
            pltpu.SemaphoreType.DMA,
            pltpu.SemaphoreType.DMA,
            pltpu.SemaphoreType.DMA((4,)),
            pltpu.SemaphoreType.DMA((4,)),
            pltpu.SemaphoreType.DMA,
            pltpu.SemaphoreType.DMA,
            pltpu.SemaphoreType.REGULAR((CHIPS,)),
        ],
        compiler_params=pltpu.CompilerParams(
            collective_id=0, has_side_effects=True, vmem_limit_bytes=64 * 2**20
        ),
        name="attend_plane",
    )(
        queries, keys, values, flags.reshape(1, rows),
        q_mask.reshape(CHIPS, HD), k_mask.reshape(CHIPS, HD), v_mask.reshape(CHIPS, HD), jnp.asarray(base), jnp.asarray(step),
    )


def solution(mesh):
    placed = (
        P(("blk", "uly"), None),
        P(("blk", "uly"), None),
        P(("blk", "uly"), None),
        P(("blk", "uly")),
        P(),
        P(),
        P(),
    )
    return jax.shard_map(
        body, mesh=mesh, in_specs=placed, out_specs=P(("blk", "uly"), None), check_vma=False
    )
```

time: 47.4 us -> 41.8 us (0.88)
  the two profiles are of different devices: /device:TPU:1 before, /device:TPU:6 now
where the time goes in v2:
time: 41.8 us; the launch traced here: 41.7 us
  Pallas kernels  40 us (96%)
  local copies, waits for them, and re-layouts  1.67 us (4%)
    pallas_call x1, Pallas kernels, body(): pl.pallas_call(functools.partial(kernel, rows), out_shape=jax.ShapeDtypeS...  40 us
    unnamed x1, local copies, waits for them, and re-layouts  1.67 us

profile of v2, /device:TPU:6, one launch (start us, length us, event | category | flops | bytes accessed | tf_op | source)
XLA Modules:
  0.0 41.7 jit_solution(5998104936549413165)
XLA Ops:
  0.0 40.0 %attend_plane.1 = bf16[32,4096]{1,0:T(8,128)(2,1)} custom-call(bf16[32,4096]{1,0:T(8,128)(2,1)} %q_hbm.1, bf16[32,4096]{1,0:T(8,128)(2,1)} %k_hbm.1, bf16[32,4096]{1,0:T(8,128)(2,1)} %v_hbm.1, s32[1,32]{1,0:T(1,128)} %bitcast.7, bf16[32,128]{1,0:T(8,128)(2,1)} %bitcast.4, bf16[32,128]{1,0:T(8,128)(2,1)} %bitcast.5, bf16[32,128]{1,0:T(8,128)(2,1)} %bitcast.6, ...), custom_call_target="tpu_custom_call" | custom-call | tf_op jit(solution)/shard_map/attend_plane/pallas_call | solution.py:220
  40.0 1.7 %copy.11 = bf16[32,4096]{1,0:T(8,128)(2,1)} copy(bf16[32,4096]{1,0:T(8,128)(2,1)} %attend_plane.1) | data formatting | bytes 524288

commit v3 on v2

--- a/solution.py
+++ b/solution.py
@@ -11,7 +11,7 @@
 
 HD = 128
 ROPE_BASE = 500000.0
-NY, NZ = 8, 4
+NX, NY, NZ = 4, 8, 4
 CHIPS = NY * NZ
 MESH = pl.DeviceIdType.MESH
 NEAR = (0, 1, 7, 2, 6, 3, 5, 4)
@@ -23,7 +23,7 @@
 
 
 def kernel(rows, q_hbm, k_hbm, v_hbm, flags_hbm, qm_hbm, km_hbm, vm_hbm, base_hbm, step_hbm, out_ref,
-           q_in, k_in, v_in, flags_ref, qm_ref, km_ref, vm_ref, base_ref, step_ref, masks, kv_stage, q_stage, kv_buf, q_buf, o_stage, o_buf,
+           q_in, k_in, v_in, flags_ref, qm_ref, km_ref, vm_ref, base_ref, step_ref, masks, kv_stage, q_stage, kv_buf, q_buf, o_stage,
            in_sem, kv_send, q_send, fwd_send, o_send, kv_recv, q_recv, fwd_recv, o_recv, ready):
     blk, uly = lax.axis_index("blk"), lax.axis_index("uly")
     blk0, y, z, core = blk // NY * NY, blk % NY, uly // 2, uly % 2
@@ -37,9 +37,11 @@
 
     def turn_of(cy, cz):
         away = jnp.minimum(cy, NY - cy)
-        late = jnp.where(cy + cz + blk0 + core == 0, 7, 0)
-        return (2 * cz + away + late) * CHIPS + cz * NY + cy
-
+        late = jnp.where(cy + cz + blk0 + core == 0, 10, 0)
+        return (z_step * cz + away + late) * CHIPS + cz * NY + cy
+
+    far_half = blk0 // (NY * NX)
+    z_step = 4 - 3 * far_half
     my_turn = turn_of(y, z)
     chips = [(cy, cz) for cz in range(NZ) for cy in range(NY)]
     turns = [turn_of(cy, cz) for cy, cz in chips]
@@ -169,9 +171,14 @@
         ).start()
     drain(kv_buf.at[:, pl.ds(half, half)], fwd_recv)
 
+    column = pl.ds(pl.multiple_of(here * HD, HD), HD)
+    spans = []
     for g in range(NZ):
-        part = pl.ds(g * group, group)
-        drain(q_buf.at[part], q_recv.at[g])
+        spans += [(g, 0, NY // 2), (g, NY // 2, NY)] if g == 0 else [(g, 0, NY)]
+    for g, y_from, y_to in spans:
+        if y_from == 0:
+            drain(q_buf.at[pl.ds(g * group, group)], q_recv.at[g])
+        part = pl.ds(g * group + y_from * rows, (y_to - y_from) * rows)
         scores = lax.dot_general(
             q_buf[part, :], kv_buf[0], (((1,), (1,)), ((), ())), preferred_element_type=jnp.float32
         )
@@ -180,29 +187,26 @@
         total = jnp.sum(weights, axis=1, keepdims=True)
         mixture = jnp.dot(weights.astype(jnp.bfloat16), kv_buf[1], preferred_element_type=jnp.float32)
         o_stage[part, :] = (mixture / total).astype(jnp.bfloat16)
-        for dy in FAR:
+        for cy in range(y_from, y_to):
+            source = pl.ds((g * NY + cy) * rows, rows)
             back = functools.partial(
-                pltpu.make_async_remote_copy, o_stage.at[slot(g * NY + y_at[dy])], o_buf.at[here], o_send, o_recv,
-                device_id=(blk0 + y_at[dy], g * 2 + core), device_id_type=MESH,
+                pltpu.make_async_remote_copy, o_stage.at[source], out_ref.at[:, column], o_send, o_recv,
+                device_id=(blk0 + cy, g * 2 + core), device_id_type=MESH,
             )
-            if dy:
+
+            @pl.when(place != g * NY + cy)
+            def _():
                 back().start()
-            else:
-                @pl.when(z != g)
-                def _():
-                    back().start()
-
-                @pl.when(z == g)
-                def _():
-                    pltpu.make_async_copy(o_stage.at[slot(place)], o_buf.at[here], o_recv).start()
+
+            @pl.when(place == g * NY + cy)
+            def _():
+                pltpu.make_async_copy(o_stage.at[source], out_ref.at[:, column], o_recv).start()
 
     others = CHIPS - 1
     drain(kv_stage.at[pl.ds(0, others)], kv_send)
     drain(q_stage.at[pl.ds(0, others)], q_send)
     drain(kv_buf.at[:, pl.ds(0, half)], fwd_send)
-    drain(o_buf, o_recv)
-    for head in range(CHIPS):
-        out_ref[:, head * HD:(head + 1) * HD] = o_buf[head]
+    drain(out_ref, o_recv)
     drain(o_stage.at[pl.ds(0, others * rows)], o_send)
 
 
@@ -219,7 +223,7 @@
     hbm = pl.BlockSpec(memory_space=pltpu.HBM)
     return pl.pallas_call(
         functools.partial(kernel, rows),
-        out_shape=jax.ShapeDtypeStruct((rows, width), jnp.bfloat16),
+        out_shape=pltpu.VMEM((rows, width), jnp.bfloat16),
         in_specs=[hbm] * 9,
         out_specs=vmem,
         scratch_shapes=[
@@ -238,7 +242,6 @@
             pltpu.VMEM((2, 2 * half, HD), jnp.bfloat16),
             pltpu.VMEM((half, HD), jnp.bfloat16),
             pltpu.VMEM((half, HD), jnp.bfloat16),
-            pltpu.VMEM((CHIPS, rows, HD), jnp.bfloat16),
             pltpu.SemaphoreType.DMA((9,)),
             pltpu.SemaphoreType.DMA,
             pltpu.SemaphoreType.DMA,
@@ -251,12 +254,14 @@
             pltpu.SemaphoreType.REGULAR((CHIPS,)),
         ],
         compiler_params=pltpu.CompilerParams(
-            collective_id=0, has_side_effects=True, vmem_limit_bytes=64 * 2**20
+            collective_id=0, has_side_effects=True, vmem_limit_bytes=48 * 2**20
         ),
         name="attend_plane",
     )(
-        queries, keys, values, flags.reshape(1, rows),
-        q_mask.reshape(CHIPS, HD), k_mask.reshape(CHIPS, HD), v_mask.reshape(CHIPS, HD), jnp.asarray(base), jnp.asarray(step),
+        *(pltpu.with_memory_space_constraint(x, pltpu.HBM) for x in (
+            queries, keys, values, flags.reshape(1, rows),
+            q_mask.reshape(CHIPS, HD), k_mask.reshape(CHIPS, HD), v_mask.reshape(CHIPS, HD), jnp.asarray(base), jnp.asarray(step),
+        ))
     )
 
 

time: 41.8 us -> 39.6 us (0.947)
  the two profiles are of different devices: /device:TPU:6 before, /device:TPU:1 now
where the time goes in v3:
time: 39.6 us; the launch traced here: 39.5 us
  Pallas kernels  38.8 us (98%)
  local copies, waits for them, and re-layouts  0.71 us (2%)
    pallas_call x1, Pallas kernels, body(): pl.pallas_call(functools.partial(kernel, rows), out_shape=pltpu.VMEM((row...  38.8 us

profile of v3, /device:TPU:1, one launch (start us, length us, event | category | flops | bytes accessed | tf_op | source)
XLA Modules:
  0.0 39.5 jit_solution(5765927751083216054)
XLA Ops:
  0.0 38.8 %attend_plane.1 = bf16[32,4096]{1,0:T(8,128)(2,1)S(1)} custom-call(bf16[32,4096]{1,0:T(8,128)(2,1)} %q_hbm.1, bf16[32,4096]{1,0:T(8,128)(2,1)} %k_hbm.1, bf16[32,4096]{1,0:T(8,128)(2,1)} %v_hbm.1, s32[1,32]{1,0:T(1,128)} %bitcast.7, bf16[32,128]{1,0:T(8,128)(2,1)} %bitcast.4, bf16[32,128]{1,0:T(8,128)(2,1)} %bitcast.5, bf16[32,128]{1,0:T(8,128)(2,1)} %bitcast.6, ...), custom_call_target="tpu_custom_call" | custom-call | tf_op jit(solution)/shard_map/attend_plane/pallas_call | solution.py:224
  38.8 0.7 %copy.11 = bf16[32,4096]{1,0:T(8,128)(2,1)} copy(bf16[32,4096]{1,0:T(8,128)(2,1)S(1)} %attend_plane.1) | data formatting | bytes 524288

commit v4 on v3

--- a/solution.py
+++ b/solution.py
@@ -17,7 +17,7 @@
 NEAR = (0, 1, 7, 2, 6, 3, 5, 4)
 FAR = NEAR[::-1]
 KV_ORDER = sorted([(dy, dz) for dy in range(NY) for dz in range(NZ)], key=lambda d: (min(d[0], NY - d[0]) + d[1], d))
-Q_ORDER = sorted([(dy, dz) for dy in range(NY) for dz in range(NZ)], key=lambda d: (min(d[0], NY - d[0]) + d[1], d))
+Q_ORDER = [(0, 0), (2, 1), (3, 3), (2, 2), (0, 1), (7, 1), (7, 3), (5, 2), (1, 0), (6, 2), (2, 0), (6, 3), (5, 3), (4, 0), (5, 1), (6, 1), (4, 1), (4, 3), (7, 2), (3, 0), (4, 2), (3, 2), (2, 3), (1, 3), (3, 1), (1, 2), (1, 1), (0, 3), (6, 0), (7, 0), (0, 2), (5, 0)]
 SENDS = [("kv", dy, dz) for dy, dz in KV_ORDER] + [("q", dy, dz) for dy, dz in Q_ORDER]
 SCALE = math.log2(math.e) / math.sqrt(HD)
 
@@ -37,11 +37,11 @@
 
     def turn_of(cy, cz):
         away = jnp.minimum(cy, NY - cy)
-        late = jnp.where(cy + cz + blk0 + core == 0, 10, 0)
+        late = jnp.where(cy + cz + blk0 + core == 0, 12, 0)
         return (z_step * cz + away + late) * CHIPS + cz * NY + cy
 
     far_half = blk0 // (NY * NX)
-    z_step = 4 - 3 * far_half
+    z_step = 2 - far_half
     my_turn = turn_of(y, z)
     chips = [(cy, cz) for cz in range(NZ) for cy in range(NY)]
     turns = [turn_of(cy, cz) for cy, cz in chips]

time: 39.6 us -> 39.4 us (level)
  no operation moved by 1% of the time
where the time goes in v4:
time: 39.4 us; the launch traced here: 39.3 us
  Pallas kernels  38.6 us (98%)
  local copies, waits for them, and re-layouts  0.71 us (2%)
    pallas_call x1, Pallas kernels, body(): pl.pallas_call(functools.partial(kernel, rows), out_shape=pltpu.VMEM((row...  38.6 us

profile of v4, /device:TPU:1, one launch (start us, length us, event | category | flops | bytes accessed | tf_op | source)
XLA Modules:
  0.0 39.3 jit_solution(6924238991763757703)
XLA Ops:
  0.0 38.6 %attend_plane.1 = bf16[32,4096]{1,0:T(8,128)(2,1)S(1)} custom-call(bf16[32,4096]{1,0:T(8,128)(2,1)} %q_hbm.1, bf16[32,4096]{1,0:T(8,128)(2,1)} %k_hbm.1, bf16[32,4096]{1,0:T(8,128)(2,1)} %v_hbm.1, s32[1,32]{1,0:T(1,128)} %bitcast.7, bf16[32,128]{1,0:T(8,128)(2,1)} %bitcast.4, bf16[32,128]{1,0:T(8,128)(2,1)} %bitcast.5, bf16[32,128]{1,0:T(8,128)(2,1)} %bitcast.6, ...), custom_call_target="tpu_custom_call" | custom-call | tf_op jit(solution)/shard_map/attend_plane/pallas_call | solution.py:224
  38.6 0.7 %copy.11 = bf16[32,4096]{1,0:T(8,128)(2,1)} copy(bf16[32,4096]{1,0:T(8,128)(2,1)S(1)} %attend_plane.1) | data formatting | bytes 524288
